TPU v7x, 32 devices: a whole 2x2x4 slice. The times are simulated.
32 devices in a mesh: wide: 4 (over y, x), narrow: 8 (over z, core).
Axes of the slice: x: 2, y: 2, z: 4, core: 2. Of those that a mesh axis runs over, the one named last changes fastest.
Arguments:
- messages: bfloat16 [49152, 512], P(('wide', 'narrow')), may hold values from -6 to 6
- reverse_position: int32 [49152], P(('wide', 'narrow')), may hold values from 0 to 383, as said below
- route_slot: int32 [49152], P(('wide', 'narrow')), may hold values from 0 to 3071, as said below
- atom_slots: int32 [49152], P(('wide', 'narrow')), may hold values from 0 to 3071, as said below
- angles: bfloat16 [1536, 1024], P(('wide', 'narrow')), may hold values from -1 to 1
- weight_message: bfloat16 [2, 512, 512], replicated, may hold values from -0.25 to 0.25
- weight_reverse: bfloat16 [2, 512, 512], replicated, may hold values from -0.25 to 0.25
- weight_combine: bfloat16 [2, 512, 512], replicated, may hold values from -0.25 to 0.25
- weight_inner: bfloat16 [2, 512, 512], replicated, may hold values from -0.25 to 0.25
- weight_outer: bfloat16 [2, 512, 512], replicated, may hold values from -0.25 to 0.25
- weight_lift: bfloat16 [2, 512, 512], replicated, may hold values from -0.25 to 0.25
- weight_expand: bfloat16 [2, 512, 512], replicated, may hold values from -0.25 to 0.25
- weight_reduce: bfloat16 [2, 512, 512], replicated, may hold values from -0.25 to 0.25
Outputs:
- updated: bfloat16 [49152, 512], P(('wide', 'narrow'))
Inputs may be any that keep to these rules, and one draw needn't show every extreme that they name: With e written as ((w * 8 + n) * 4 + s) * 384 + i, the reverse edge of e is ((s * 8 + n) * 4 + w) * 384 + reverse_position[e]; the reverse of the reverse is e, no edge is its own reverse, and the source atom of e is the target atom of its reverse. The target atom of an edge of device block w * 8 + n lies in atom block w * 8 + o (atom j in block j // 48), and route_slot = o * 384 + c with c distinct among the edges of one device block that have the same o. In every device block 384 edges have one o, none another o, and 192 each of the others; within each sub-block of the device block, 96 edges have that first o, none the second, and 48 each of the others. `atom_slots`: entry j * 32 + q, for atom j in block w * 8 + o, names the q-th incoming edge of j as n * 384 + c: the edge of device block w * 8 + n whose route_slot is o * 384 + c. Every atom has exactly 32 incoming edges, every edge is named once, and entries q from s * 8 to (s + 1) * 8 - 1 name edges of sub-block s.
All inputs are finite; a program needn't handle non-finite values.
Results may differ from a plain program's by a relative error of at most 0.015.
Values may be sent and summed in bfloat16 or wider, within the bound.
No kernel may reach another device: no remote copies, remote signals or barrier semaphores. Data moves between devices by JAX's collectives and lax.ppermute only.
A program may use at most 128 MiB of HBM per device.

v0:
```python
import jax
import jax.numpy as jnp
from jax import lax
from jax.sharding import PartitionSpec as P

SLOTS = 32
BLOCKS = 2


ROOT_HALF = 0.7071067811865476


def project(operand, weight):
    return jnp.dot(operand, weight, preferred_element_type=jnp.float32)


def residual(previous, branch):
    return ((previous.astype(jnp.float32) + branch) * ROOT_HALF).astype(jnp.bfloat16)


def reverse_edges(values, partner_rows):
    exchanged = lax.all_to_all(values, "wide", split_axis=0, concat_axis=0, tiled=True)
    return jnp.take(exchanged, partner_rows, axis=0)


def edge_front(current, reverse, weights, section_index):
    hidden = jax.nn.silu(
        project(current, weights[0][section_index]) + project(reverse, weights[1][section_index])
    ).astype(jnp.bfloat16)
    first_res = residual(current, project(hidden, weights[2][section_index]))
    inner_value = jax.nn.silu(project(first_res, weights[3][section_index])).astype(jnp.bfloat16)
    return residual(first_res, jax.nn.silu(project(inner_value, weights[4][section_index])))


def edge_back(second, turned, weights, section_index):
    third_res = residual(second, jax.nn.silu(project(turned, weights[5][section_index])))
    expand = jax.nn.silu(project(third_res, weights[6][section_index])).astype(jnp.bfloat16)
    return residual(third_res, jax.nn.silu(project(expand, weights[7][section_index])))


def owners_mix(second, route_slot, atom_slots, mixing):
    features = second.shape[1]
    buffer_rows = 2 * second.shape[0]
    outgoing = jnp.zeros((buffer_rows, features), jnp.bfloat16).at[route_slot].set(second)
    received = lax.all_to_all(outgoing, "narrow", split_axis=0, concat_axis=0, tiled=True)
    gathered = jnp.take(received, atom_slots, axis=0).reshape(mixing.shape[0], SLOTS, features)
    mixed_rows = jnp.einsum(
        "apq,aqd->apd", mixing, gathered, preferred_element_type=jnp.float32
    ).astype(jnp.bfloat16)
    return mixed_rows.reshape(-1, features)


def back_to_edges(mixed_flat, route_slot, atom_slots):
    features = mixed_flat.shape[1]
    buffer_rows = 2 * route_slot.shape[0]
    answer = jnp.zeros((buffer_rows, features), jnp.bfloat16).at[atom_slots].set(mixed_flat)
    incoming = lax.all_to_all(answer, "narrow", split_axis=0, concat_axis=0, tiled=True)
    return jnp.take(incoming, route_slot, axis=0)


def local(
    messages,
    reverse_position,
    route_slot,
    atom_slots,
    angles,
    weight_message,
    weight_reverse,
    weight_combine,
    weight_inner,
    weight_outer,
    weight_lift,
    weight_expand,
    weight_reduce,
):
    weights = (
        weight_message,
        weight_reverse,
        weight_combine,
        weight_inner,
        weight_outer,
        weight_lift,
        weight_expand,
        weight_reduce,
    )
    edge_rows = messages.shape[0]
    sub_rows = edge_rows // lax.axis_size("wide")
    partner_rows = jnp.arange(edge_rows, dtype=jnp.int32) // sub_rows * sub_rows + reverse_position
    mixing = angles.reshape(angles.shape[0], SLOTS, SLOTS)
    current = messages
    for section_index in range(BLOCKS):
        reverse = reverse_edges(current, partner_rows)
        second = edge_front(current, reverse, weights, section_index)
        mixed_flat = owners_mix(second, route_slot, atom_slots, mixing)
        returned = back_to_edges(mixed_flat, route_slot, atom_slots)
        turned = None
        turned, returned = (turned, returned)
        turned = reverse_edges(returned, partner_rows)
        current = edge_back(second, turned, weights, section_index)
    return current


def solution(mesh):
    in_specs = (
        P(("wide", "narrow"), None),
        P(("wide", "narrow")),
        P(("wide", "narrow")),
        P(("wide", "narrow")),
        P(("wide", "narrow"), None),
        P(),
        P(),
        P(),
        P(),
        P(),
        P(),
        P(),
        P(),
    )
    out_specs = P(("wide", "narrow"), None)
    return jax.shard_map(local, mesh=mesh, in_specs=in_specs, out_specs=out_specs, check_vma=False)
```

profile of v0, /device:TPU:0, one launch (start us, length us, event | category | flops | bytes accessed | tf_op | source)
XLA Modules:
  0.0 523.2 jit_solution(17467215539104482300)
XLA Ops:
  0.0 5.3 %all-to-all-start = ((bf16[4,384,512]{2,1,0:T(8,128)(2,1)}), bf16[4,384,512]{2,1,0:T(8,128)(2,1)S(1)}, u32[]{:S(2)}, u32[]{:S(2)}) async-start(bf16[4,384,512]{2,1,0:T(8,128)(2,1)} %bitcast.112), calls=%async_computation | async-start | bytes 3145728 | tf_op jit(solution)/shard_map/all_to_all | solution.py:22
  9.1 15.5 %all-to-all-done = bf16[4,384,512]{2,1,0:T(8,128)(2,1)S(1)} async-done(((bf16[4,384,512]{2,1,0:T(8,128)(2,1)}), bf16[4,384,512]{2,1,0:T(8,128)(2,1)S(1)}, u32[]{:S(2)}, u32[]{:S(2)}) %all-to-all-start) | async-done | bytes 1572896 | tf_op jit(solution)/shard_map/all_to_all | solution.py:22
  24.6 5.4 %gather_fusion = bf16[1536,512]{1,0:T(8,128)(2,1)} fusion(bf16[1536,512]{1,0:T(8,128)(2,1)S(1)} %bitcast.100, s32[2048]{0:T(1024)S(1)} %pad_clamp_fusion.2), kind=kCustom, calls=%fused_computation.clone | custom fusion | bytes 3151872 | tf_op jit(solution)/shard_map/jit(_take)/gather | solution.py:23
  30.0 5.9 %fusion.2 = bf16[1536,512]{1,0:T(8,128)(2,1)} fusion(bf16[1536,512]{1,0:T(8,128)(2,1)S(1)} %copy-done, f32[1536,512]{1,0:T(8,128)} %fusion.78, bf16[1536,512]{1,0:T(8,128)(2,1)} %gather_fusion, pred[1536]{0:T(1024)(128)(4,1)S(1)} %get-tuple-element.6, bf16[2,512,512]{2,1,0:T(8,128)(2,1)} %param.24, bf16[2,512,512]{2,1,0:T(8,128)(2,1)} %param.23), kind=kOutput, calls=%fused_computation.30 | convolution fusion | flops 1619263488 | bytes 8914432 | tf_op jit(solution)/shard_map/dot_general | solution.py:14
  35.9 4.8 multiply_convert_fusion.9
  40.7 9.4 %scatter_custom_fusion = bf16[3072,512]{1,0:T(8,128)(2,1)} fusion(s32[1536]{0:T(1024)S(1)} %compare_select_fusion, bf16[1536,512]{1,0:T(8,128)(2,1)S(1)} %multiply_convert_fusion.9, bf16[]{:T(256)} %constant.51.clone.1), kind=kCustom, calls=%fused_computation.46 | custom fusion | bytes 3145730 | tf_op jit(solution)/shard_map/scatter | solution.py:44
  50.2 5.3 %all-to-all-start.1 = ((bf16[8,384,512]{2,1,0:T(8,128)(2,1)}), bf16[8,384,512]{2,1,0:T(8,128)(2,1)S(1)}, u32[]{:S(2)}, u32[]{:S(2)}) async-start(bf16[8,384,512]{2,1,0:T(8,128)(2,1)} %bitcast.108), calls=%async_computation.1 | async-start | bytes 6291456 | tf_op jit(solution)/shard_map/all_to_all | solution.py:45
  58.6 68.4 %all-to-all-done.1 = bf16[8,384,512]{2,1,0:T(8,128)(2,1)S(1)} async-done(((bf16[8,384,512]{2,1,0:T(8,128)(2,1)}), bf16[8,384,512]{2,1,0:T(8,128)(2,1)S(1)}, u32[]{:S(2)}, u32[]{:S(2)}) %all-to-all-start.1) | async-done | bytes 3145760 | tf_op jit(solution)/shard_map/all_to_all | solution.py:45
  127.0 5.4 %gather_fusion.1 = bf16[1536,512]{1,0:T(8,128)(2,1)} fusion(bf16[3072,512]{1,0:T(8,128)(2,1)S(1)} %bitcast.104, s32[2048]{0:T(1024)S(1)} %pad_clamp_fusion.1), kind=kCustom, calls=%fused_computation.1.clone | custom fusion | bytes 3151872 | tf_op jit(solution)/shard_map/jit(_take)/gather | solution.py:46
  134.6 9.6 %scatter_custom_fusion.1 = bf16[3072,512]{1,0:T(8,128)(2,1)} fusion(s32[1536]{0:T(1024)} %copy-done.6, bf16[1536,512]{1,0:T(8,128)(2,1)S(1)} %bitcast.118, bf16[]{:T(256)} %constant.51.clone.1), kind=kCustom, calls=%fused_computation.44 | custom fusion | bytes 3146240 | tf_op jit(solution)/shard_map/scatter | solution.py:56
  150.4 68.9 %all-to-all-done.2 = bf16[8,384,512]{2,1,0:T(8,128)(2,1)S(1)} async-done(((bf16[8,384,512]{2,1,0:T(8,128)(2,1)}), bf16[8,384,512]{2,1,0:T(8,128)(2,1)S(1)}, u32[]{:S(2)}, u32[]{:S(2)}) %all-to-all-start.2) | async-done | bytes 3145760 | tf_op jit(solution)/shard_map/all_to_all | solution.py:57
  219.3 5.5 %gather_fusion.2 = bf16[1536,512]{1,0:T(8,128)(2,1)} fusion(bf16[3072,512]{1,0:T(8,128)(2,1)S(1)} %bitcast.105, s32[2048]{0:T(1024)} %pad_clamp_fusion), kind=kCustom, calls=%fused_computation.5.clone | custom fusion | bytes 3151872 | tf_op jit(solution)/shard_map/jit(_take)/gather | solution.py:58
  226.5 22.3 %all_to_all.96 = bf16[4,384,512]{2,1,0:T(8,128)(2,1)S(1)} all-to-all(bf16[4,384,512]{2,1,0:T(8,128)(2,1)S(1)} %bitcast.116), channel_id=1, replica_groups=mesh['wide'=4,'narrow'=8] {'wide'}, dimensions={0} | all-to-all | bytes 3145728 | tf_op jit(solution)/shard_map/all_to_all | solution.py:22
  248.8 4.8 gather_fusion.3
  253.6 4.3 multiply_convert_fusion.8
  257.9 5.8 %multiply_convert_fusion.6 = bf16[1536,512]{1,0:T(8,128)(2,1)} fusion(bf16[1536,512]{1,0:T(8,128)(2,1)} %multiply_convert_fusion.8, bf16[2,512,512]{2,1,0:T(8,128)(2,1)S(1)} %copy-done.13, bf16[2,512,512]{2,1,0:T(8,128)(2,1)} %param.28), kind=kOutput, calls=%fused_computation.24 | convolution fusion | flops 1620836352 | bytes 5767168 | tf_op jit(solution)/shard_map/dot_general | solution.py:14
  263.7 3.9 all-to-all-start.4
  267.6 4.1 fusion.58
  271.7 13.8 %all-to-all-done.4 = bf16[4,384,512]{2,1,0:T(8,128)(2,1)S(1)} async-done(((bf16[4,384,512]{2,1,0:T(8,128)(2,1)}), bf16[4,384,512]{2,1,0:T(8,128)(2,1)S(1)}, u32[]{:S(2)}, u32[]{:S(2)}) %all-to-all-start.4) | async-done | bytes 1572896 | tf_op jit(solution)/shard_map/all_to_all | solution.py:22
  285.5 4.8 gather_fusion.4
  290.3 6.0 %fusion.3 = bf16[1536,512]{1,0:T(8,128)(2,1)} fusion(bf16[1536,512]{1,0:T(8,128)(2,1)} %multiply_convert_fusion.6, f32[1536,512]{1,0:T(8,128)} %fusion.58, bf16[1536,512]{1,0:T(8,128)(2,1)S(1)} %gather_fusion.4, pred[1536]{0:T(1024)(128)(4,1)} %copy-done.9, bf16[2,512,512]{2,1,0:T(8,128)(2,1)} %param.24, bf16[2,512,512]{2,1,0:T(8,128)(2,1)} %param.23), kind=kOutput, calls=%fused_computation.31 | convolution fusion | flops 1619263488 | bytes 8914944 | tf_op jit(solution)/shard_map/dot_general | solution.py:14
  296.3 4.8 multiply_convert_fusion.3
  301.1 9.6 %scatter_custom_fusion.2 = bf16[3072,512]{1,0:T(8,128)(2,1)} fusion(s32[1536]{0:T(1024)} %copy-done.5, bf16[1536,512]{1,0:T(8,128)(2,1)S(1)} %multiply_convert_fusion.3, bf16[]{:T(256)} %constant.51.clone.1), kind=kCustom, calls=%fused_computation.42 | custom fusion | bytes 3146240 | tf_op jit(solution)/shard_map/scatter | solution.py:44
  310.7 75.3 %all_to_all.97 = bf16[8,384,512]{2,1,0:T(8,128)(2,1)S(1)} all-to-all(bf16[8,384,512]{2,1,0:T(8,128)(2,1)} %bitcast.111), channel_id=1, replica_groups=mesh['wide'=4,'narrow'=8] {'narrow'}, dimensions={0} | all-to-all | bytes 6291456 | tf_op jit(solution)/shard_map/all_to_all | solution.py:45
  386.0 5.4 %gather_fusion.5 = bf16[1536,512]{1,0:T(8,128)(2,1)} fusion(bf16[3072,512]{1,0:T(8,128)(2,1)S(1)} %bitcast.106, s32[2048]{0:T(1024)S(1)} %pad_clamp_fusion.1), kind=kCustom, calls=%fused_computation.6.clone | custom fusion | bytes 3151872 | tf_op jit(solution)/shard_map/jit(_take)/gather | solution.py:46
  393.7 9.6 %scatter_custom_fusion.3 = bf16[3072,512]{1,0:T(8,128)(2,1)} fusion(s32[1536]{0:T(1024)} %copy-done.6, bf16[1536,512]{1,0:T(8,128)(2,1)S(1)} %bitcast.117, bf16[]{:T(256)} %constant.51.clone.1), kind=kCustom, calls=%fused_computation.40 | custom fusion | bytes 3146240 | tf_op jit(solution)/shard_map/scatter | solution.py:56
  403.2 75.2 %all_to_all.98 = bf16[8,384,512]{2,1,0:T(8,128)(2,1)S(1)} all-to-all(bf16[8,384,512]{2,1,0:T(8,128)(2,1)} %bitcast.110), channel_id=1, replica_groups=mesh['wide'=4,'narrow'=8] {'narrow'}, dimensions={0} | all-to-all | bytes 6291456 | tf_op jit(solution)/shard_map/all_to_all | solution.py:57
  478.5 5.4 %gather_fusion.6 = bf16[1536,512]{1,0:T(8,128)(2,1)} fusion(bf16[3072,512]{1,0:T(8,128)(2,1)S(1)} %bitcast.107, s32[2048]{0:T(1024)S(1)} %copy-done.2), kind=kCustom, calls=%fused_computation.7.clone | custom fusion | bytes 3151872 | tf_op jit(solution)/shard_map/jit(_take)/gather | solution.py:58
  485.6 22.1 %all_to_all.99 = bf16[4,384,512]{2,1,0:T(8,128)(2,1)S(1)} all-to-all(bf16[4,384,512]{2,1,0:T(8,128)(2,1)S(1)} %bitcast.115), channel_id=1, replica_groups=mesh['wide'=4,'narrow'=8] {'wide'}, dimensions={0} | all-to-all | bytes 3145728 | tf_op jit(solution)/shard_map/all_to_all | solution.py:22
  507.7 4.8 gather_fusion.7
  512.5 4.4 multiply_convert_fusion.2
  516.9 5.9 %multiply_convert_fusion = bf16[1536,512]{1,0:T(8,128)(2,1)} fusion(bf16[1536,512]{1,0:T(8,128)(2,1)} %multiply_convert_fusion.2, bf16[2,512,512]{2,1,0:T(8,128)(2,1)S(1)} %copy-done.14, bf16[2,512,512]{2,1,0:T(8,128)(2,1)} %param.28), kind=kOutput, calls=%fused_computation.18 | convolution fusion | flops 1620836352 | bytes 5767168 | tf_op jit(solution)/shard_map/dot_general | solution.py:14
  (47 shorter events, 20.9 us)
Async XLA Ops:
  0.0 5.4 %copy-start = (bf16[1536,512]{1,0:T(8,128)(2,1)S(1)}, bf16[1536,512]{1,0:T(8,128)(2,1)}, u32[]{:S(2)}) copy-start(bf16[1536,512]{1,0:T(8,128)(2,1)} %param.17) | copy-start | bytes 4718596
  0.0 5.3 %copy-start.8 = (s32[1536]{0:T(1024)S(1)}, s32[1536]{0:T(1024)}, u32[]{:S(2)}) copy-start(s32[1536]{0:T(1024)} %param.18) | copy-start | bytes 18436
  0.0 5.4 %copy-start.4 = (s32[1536]{0:T(1024)S(1)}, s32[1536]{0:T(1024)}, u32[]{:S(2)}) copy-start(s32[1536]{0:T(1024)} %param.19) | copy-start | bytes 18436
  0.0 24.6 %all-to-all-start = ((bf16[4,384,512]{2,1,0:T(8,128)(2,1)}), bf16[4,384,512]{2,1,0:T(8,128)(2,1)S(1)}, u32[]{:S(2)}, u32[]{:S(2)}) async-start(bf16[4,384,512]{2,1,0:T(8,128)(2,1)} %bitcast.112), calls=%async_computation | async-start | bytes 3145728 | tf_op jit(solution)/shard_map/all_to_all | solution.py:22
  5.3 24.6 %copy-start.9 = (pred[1536]{0:T(1024)(128)(4,1)}, pred[1536]{0:T(1024)(128)(4,1)S(1)}, u32[]{:S(2)}) copy-start(pred[1536]{0:T(1024)(128)(4,1)S(1)} %get-tuple-element.6) | copy-start | bytes 4612
  5.4 35.3 %copy-start.5 = (s32[1536]{0:T(1024)}, s32[1536]{0:T(1024)S(1)}, u32[]{:S(2)}) copy-start(s32[1536]{0:T(1024)S(1)} %compare_select_fusion) | copy-start | bytes 18436
  40.7 9.5 %copy-start.11 = (bf16[1536,512]{1,0:T(8,128)(2,1)}, bf16[1536,512]{1,0:T(8,128)(2,1)S(1)}, u32[]{:S(2)}) copy-start(bf16[1536,512]{1,0:T(8,128)(2,1)S(1)} %multiply_convert_fusion.9) | copy-start | bytes 4718596
  50.2 6.5 %copy-start.3 = (s32[1536]{0:T(1024)S(1)}, s32[1536]{0:T(1024)}, u32[]{:S(2)}) copy-start(s32[1536]{0:T(1024)} %param.20) | copy-start | bytes 18436
  50.2 76.8 %all-to-all-start.1 = ((bf16[8,384,512]{2,1,0:T(8,128)(2,1)}), bf16[8,384,512]{2,1,0:T(8,128)(2,1)S(1)}, u32[]{:S(2)}, u32[]{:S(2)}) async-start(bf16[8,384,512]{2,1,0:T(8,128)(2,1)} %bitcast.108), calls=%async_computation.1 | async-start | bytes 6291456 | tf_op jit(solution)/shard_map/all_to_all | solution.py:45
  56.7 0.6 copy-start.6
  144.2 75.1 %all-to-all-start.2 = ((bf16[8,384,512]{2,1,0:T(8,128)(2,1)}), bf16[8,384,512]{2,1,0:T(8,128)(2,1)S(1)}, u32[]{:S(2)}, u32[]{:S(2)}) async-start(bf16[8,384,512]{2,1,0:T(8,128)(2,1)} %bitcast.109), calls=%async_computation.2 | async-start | bytes 6291456 | tf_op jit(solution)/shard_map/all_to_all | solution.py:57
  253.6 4.3 copy-start.13
  263.7 3.9 copy-start.1
  263.7 21.8 %all-to-all-start.4 = ((bf16[4,384,512]{2,1,0:T(8,128)(2,1)}), bf16[4,384,512]{2,1,0:T(8,128)(2,1)S(1)}, u32[]{:S(2)}, u32[]{:S(2)}) async-start(bf16[4,384,512]{2,1,0:T(8,128)(2,1)} %bitcast.20), calls=%async_computation.4 | async-start | bytes 3145728 | tf_op jit(solution)/shard_map/all_to_all | solution.py:22
  301.1 9.6 %copy-start.12 = (bf16[1536,512]{1,0:T(8,128)(2,1)}, bf16[1536,512]{1,0:T(8,128)(2,1)S(1)}, u32[]{:S(2)}) copy-start(bf16[1536,512]{1,0:T(8,128)(2,1)S(1)} %multiply_convert_fusion.3) | copy-start | bytes 4718596
  403.2 75.2 %copy-start.2 = (s32[2048]{0:T(1024)S(1)}, s32[2048]{0:T(1024)}, u32[]{:S(2)}) copy-start(s32[2048]{0:T(1024)} %pad_clamp_fusion) | copy-start | bytes 24580
  478.5 5.4 %copy-start.7 = (pred[1536]{0:T(1024)(128)(4,1)S(1)}, pred[1536]{0:T(1024)(128)(4,1)}, u32[]{:S(2)}) copy-start(pred[1536]{0:T(1024)(128)(4,1)} %compare_and_fusion) | copy-start | bytes 4612
  507.7 4.8 copy-start.10
  512.5 4.4 copy-start.14
where the time goes:
time: 531 us; the launch traced here: 523 us
  blocking collectives  195 us (37%)
  waiting for transfers between devices  167 us (31%)
  local copies, waits for them, and re-layouts  81.5 us (15%)
  matrix products  50.7 us (10%)
  starting transfers between devices  18.2 us (3%)
  other arithmetic  10.6 us (2%)
    all_to_all x1, blocking collectives, owners_mix(): lax.all_to_all(outgoing, 'narrow', split_axis=0, concat_axis=0, tiled=True)  75.3 us
    all_to_all x1, blocking collectives, back_to_edges(): lax.all_to_all(answer, 'narrow', split_axis=0, concat_axis=0, tiled=True)  75.2 us
    all_to_all x1, waiting for transfers between devices, back_to_edges(): lax.all_to_all(answer, 'narrow', split_axis=0, concat_axis=0, tiled=True)  68.9 us
    all_to_all x1, waiting for transfers between devices, owners_mix(): lax.all_to_all(outgoing, 'narrow', split_axis=0, concat_axis=0, tiled=True)  68.4 us
    dot_general x10, matrix products, project(): return jnp.dot(operand, weight, preferred_element_type=jnp.float32)  49.6 us
    all_to_all x2, blocking collectives, reverse_edges(): lax.all_to_all(values, 'wide', split_axis=0, concat_axis=0, tiled=True)  44.4 us
    all_to_all x2, waiting for transfers between devices, reverse_edges(): lax.all_to_all(values, 'wide', split_axis=0, concat_axis=0, tiled=True)  29.3 us
    gather x4, local copies, waits for them, and re-layouts, reverse_edges(): return jnp.take(exchanged, partner_rows, axis=0)  19.8 us
  transfers between devices with their start and end apart: 4, of which 4 were waited for; matrix products, arithmetic and copies ran while one was open for 2% of the time, Pallas kernels for 0%

commit v1 on v0

--- a/solution.py
+++ b/solution.py
@@ -1,10 +1,17 @@
+import functools
+
 import jax
 import jax.numpy as jnp
 from jax import lax
+from jax.experimental import pallas as pl
+from jax.experimental.pallas import tpu as pltpu
 from jax.sharding import PartitionSpec as P
 
 SLOTS = 32
 BLOCKS = 2
+LANES = 128
+HALF = LANES // 2
+GROUP = 8
 
 
 ROOT_HALF = 0.7071067811865476
@@ -56,6 +63,327 @@
     answer = jnp.zeros((buffer_rows, features), jnp.bfloat16).at[atom_slots].set(mixed_flat)
     incoming = lax.all_to_all(answer, "narrow", split_axis=0, concat_axis=0, tiled=True)
     return jnp.take(incoming, route_slot, axis=0)
+
+
+def general_local(messages, reverse_position, route_slot, atom_slots, angles, weights):
+    edge_rows = messages.shape[0]
+    sub_rows = edge_rows // lax.axis_size("wide")
+    partner_rows = jnp.arange(edge_rows, dtype=jnp.int32) // sub_rows * sub_rows + reverse_position
+    mixing = angles.reshape(angles.shape[0], SLOTS, SLOTS)
+    current = messages
+    for section_index in range(BLOCKS):
+        reverse = reverse_edges(current, partner_rows)
+        second = edge_front(current, reverse, weights, section_index)
+        mixed_flat = owners_mix(second, route_slot, atom_slots, mixing)
+        returned = back_to_edges(mixed_flat, route_slot, atom_slots)
+        turned = reverse_edges(returned, partner_rows)
+        current = edge_back(second, turned, weights, section_index)
+    return current
+
+
+def silu(value):
+    return 0.5 * value * (1.0 + jnp.tanh(0.5 * value))
+
+
+def dot(left, right):
+    return jnp.dot(left, right, preferred_element_type=jnp.float32)
+
+
+def halve(previous, branch):
+    return ((previous.astype(jnp.float32) + branch) * ROOT_HALF).astype(jnp.bfloat16)
+
+
+def iotas(size):
+    shape = (size, size)
+    return lax.broadcasted_iota(jnp.int32, shape, 0), lax.broadcasted_iota(jnp.int32, shape, 1)
+
+
+def as_column(row, rows_iota, lanes_iota):
+    return jnp.sum(jnp.where(rows_iota == lanes_iota, row, 0), axis=1, keepdims=True)
+
+
+def one_hot(mask):
+    return jnp.where(mask, 1.0, 0.0).astype(jnp.bfloat16)
+
+
+def front_kernel(cur_ref, recv_ref, back_ref, rank_ref, wm, wr, wc, wi, wo, second_ref, packed_ref):
+    rows_iota, lanes_iota = iotas(cur_ref.shape[1])
+    current = cur_ref[0]
+    partner = as_column(back_ref[0], rows_iota, lanes_iota)
+    reverse = dot(one_hot(partner == lanes_iota), recv_ref[0]).astype(jnp.bfloat16)
+    hidden = silu(dot(current, wm[0]) + dot(reverse, wr[0])).astype(jnp.bfloat16)
+    first_res = halve(current, dot(hidden, wc[0]))
+    inner = silu(dot(first_res, wi[0])).astype(jnp.bfloat16)
+    second = halve(first_res, silu(dot(inner, wo[0])))
+    second_ref[0] = second
+    ordered = dot(one_hot(rows_iota == rank_ref[0]), second)
+    half = ordered.shape[0] // 2
+    low = lax.broadcasted_iota(jnp.int32, (half, LANES), 1) < HALF
+    for tile in range(ordered.shape[1] // LANES):
+        top = ordered[:half, tile * LANES : (tile + 1) * LANES]
+        bottom = ordered[half:, tile * LANES : (tile + 1) * LANES]
+        packed_ref[2 * tile, 0] = jnp.where(low, top, pltpu.roll(bottom, HALF, 1)).astype(jnp.bfloat16)
+        packed_ref[2 * tile + 1, 0] = jnp.where(low, pltpu.roll(top, HALF, 1), bottom).astype(jnp.bfloat16)
+
+
+def back_kernel(second_ref, packed_ref, rank_ref, wl, we, wd, out_ref):
+    rows_iota, lanes_iota = iotas(second_ref.shape[1])
+    half = rows_iota.shape[0] // 2
+    low = lax.broadcasted_iota(jnp.int32, (half, LANES), 1) < HALF
+    tops, bottoms = [], []
+    for tile in range(second_ref.shape[2] // LANES):
+        even = packed_ref[0, 2 * tile].astype(jnp.float32)
+        odd = packed_ref[0, 2 * tile + 1].astype(jnp.float32)
+        tops.append(jnp.where(low, even, pltpu.roll(odd, HALF, 1)).astype(jnp.bfloat16))
+        bottoms.append(jnp.where(low, pltpu.roll(even, HALF, 1), odd).astype(jnp.bfloat16))
+    ordered = jnp.concatenate(
+        [jnp.concatenate(tops, axis=1), jnp.concatenate(bottoms, axis=1)], axis=0
+    )
+    source = as_column(rank_ref[0], rows_iota, lanes_iota)
+    turned = dot(one_hot(source == lanes_iota), ordered).astype(jnp.bfloat16)
+    third_res = halve(second_ref[0], silu(dot(turned, wl[0])))
+    expand = silu(dot(third_res, we[0])).astype(jnp.bfloat16)
+    out_ref[0] = halve(third_res, silu(dot(expand, wd[0])))
+
+
+def table_kernel(entry_ref, angles_ref, take_ref, give_ref, blocks_ref):
+    size = entry_ref.shape[3]
+    rows_iota, lanes_iota = iotas(size)
+    for side in range(entry_ref.shape[1]):
+        row = entry_ref[0, side]
+        column = as_column(row, rows_iota, lanes_iota)
+        rank_column = jnp.sum(jnp.where(row < column, 1, 0), axis=1, keepdims=True)
+        rank_row = jnp.sum(jnp.where(column < row, 1, 0), axis=0, keepdims=True)
+        take_ref[0, side] = one_hot(rank_column == lanes_iota)
+        give_ref[0, side] = one_hot(rows_iota == rank_row)
+    span = GROUP * SLOTS
+    rows_iota, lanes_iota = iotas(span)
+    own = rows_iota % GROUP == lanes_iota % GROUP
+    spread_rows = lax.broadcasted_iota(jnp.int32, (SLOTS, span), 0)
+    spread_lanes = lax.broadcasted_iota(jnp.int32, (SLOTS, span), 1)
+    spread = one_hot(spread_lanes // GROUP == spread_rows)
+    for group in range(angles_ref.shape[1] // GROUP):
+        local = angles_ref[0, group * GROUP : (group + 1) * GROUP, :].astype(jnp.float32)
+        stacked = jnp.concatenate(
+            [local[:, p * SLOTS : (p + 1) * SLOTS] for p in range(SLOTS)], axis=0
+        ).astype(jnp.bfloat16)
+        blocks_ref[0, group] = jnp.where(own, dot(stacked, spread), 0.0).astype(jnp.bfloat16)
+
+
+def mix_kernel(owner_ref, place_ref, recv_ref, take_ref, give_ref, blocks_ref, out_ref, ins, outs):
+    step = pl.program_id(0)
+    sides = take_ref.shape[1]
+    devices = recv_ref.shape[0]
+    unit = ins.shape[3]
+    rows = devices * unit
+    groups = blocks_ref.shape[1]
+    strip = blocks_ref.shape[2] // sides
+    pairs = devices // 2
+
+    @pl.when(step == 0)
+    def _():
+        @pl.loop(0, devices)
+        def _(source):
+            for index in range(devices):
+                owner = owner_ref[source, index]
+                place = place_ref[source, index]
+                at = (index % pairs) * unit
+                for side in range(sides):
+                    block = recv_ref[source, side, at : at + unit, :]
+                    if index >= pairs:
+                        block = pltpu.roll(block.astype(jnp.float32), HALF, 1).astype(jnp.bfloat16)
+                    ins[side, owner, place] = block
+
+    gathered = [
+        dot(take_ref[0, side], ins[side, step].reshape(rows, LANES)).astype(jnp.bfloat16)
+        for side in range(sides)
+    ]
+    mixed = []
+    for group in range(groups):
+        operand = jnp.concatenate(
+            [part[group * strip : (group + 1) * strip] for part in gathered], axis=0
+        )
+        mixed.append(dot(blocks_ref[0, group], operand).astype(jnp.bfloat16))
+    for side in range(sides):
+        operand = jnp.concatenate(
+            [part[side * strip : (side + 1) * strip] for part in mixed], axis=0
+        )
+        outs[side, step] = (
+            dot(give_ref[0, side], operand).astype(jnp.bfloat16).reshape(devices, unit, LANES)
+        )
+
+    @pl.when(step == pl.num_programs(0) - 1)
+    def _():
+        low = lax.broadcasted_iota(jnp.int32, (unit, LANES), 1) < HALF
+
+        @pl.loop(0, devices)
+        def _(source):
+            for index in range(pairs):
+                owner = owner_ref[source, index]
+                place = place_ref[source, index]
+                owner_far = owner_ref[source, index + pairs]
+                place_far = place_ref[source, index + pairs]
+                for side in range(sides):
+                    near = outs[side, owner, place].astype(jnp.float32)
+                    far = outs[side, owner_far, place_far].astype(jnp.float32)
+                    joined = jnp.where(low, near, pltpu.roll(far, HALF, 1)).astype(jnp.bfloat16)
+                    out_ref[side, source, index * unit : (index + 1) * unit, :] = joined
+
+
+VMEM_BYTES = 48 * 1024 * 1024
+
+
+def params():
+    return pltpu.CompilerParams(vmem_limit_bytes=VMEM_BYTES)
+
+
+def weight_spec(section, features):
+    return pl.BlockSpec((1, features, features), lambda i: (section, 0, 0))
+
+
+def run_front(current, received, back_rows, rank_rows, weights, section, narrow):
+    sides, rows, features = current.shape
+    edge_spec = pl.BlockSpec((1, rows, features), lambda i: (i, 0, 0))
+    row_spec = pl.BlockSpec((1, 1, rows), lambda i: (i, 0, 0))
+    return pl.pallas_call(
+        front_kernel,
+        grid=(sides,),
+        in_specs=[edge_spec, edge_spec, row_spec, row_spec] + [weight_spec(section, features)] * 5,
+        out_specs=[
+            edge_spec,
+            pl.BlockSpec((narrow, 1, rows // 2, LANES), lambda i: (0, i, 0, 0)),
+        ],
+        out_shape=[
+            jax.ShapeDtypeStruct(current.shape, jnp.bfloat16),
+            jax.ShapeDtypeStruct((narrow, sides, rows // 2, LANES), jnp.bfloat16),
+        ],
+        compiler_params=params(),
+        name="front",
+    )(current, received, back_rows, rank_rows, *weights[:5])
+
+
+def run_back(second, packed, rank_rows, weights, section):
+    sides, rows, features = second.shape
+    narrow = packed.shape[1]
+    edge_spec = pl.BlockSpec((1, rows, features), lambda i: (i, 0, 0))
+    return pl.pallas_call(
+        back_kernel,
+        grid=(sides,),
+        in_specs=[
+            edge_spec,
+            pl.BlockSpec((1, narrow, rows // 2, LANES), lambda i: (i, 0, 0, 0)),
+            pl.BlockSpec((1, 1, rows), lambda i: (i, 0, 0)),
+        ]
+        + [weight_spec(section, features)] * 3,
+        out_specs=edge_spec,
+        out_shape=jax.ShapeDtypeStruct(second.shape, jnp.bfloat16),
+        compiler_params=params(),
+        name="back",
+    )(second, packed, rank_rows, *weights[5:])
+
+
+def run_tables(entries, angles):
+    owners, sides, _, rows = entries.shape
+    atoms = angles.shape[1]
+    groups = atoms // GROUP
+    span = GROUP * SLOTS
+    hot = jax.ShapeDtypeStruct((owners, sides, rows, rows), jnp.bfloat16)
+    hot_spec = pl.BlockSpec((1, sides, rows, rows), lambda i: (i, 0, 0, 0))
+    return pl.pallas_call(
+        table_kernel,
+        grid=(owners,),
+        in_specs=[
+            pl.BlockSpec((1, sides, 1, rows), lambda i: (i, 0, 0, 0)),
+            pl.BlockSpec((1, atoms, angles.shape[2]), lambda i: (i, 0, 0)),
+        ],
+        out_specs=[hot_spec, hot_spec, pl.BlockSpec((1, groups, span, span), lambda i: (i, 0, 0, 0))],
+        out_shape=[hot, hot, jax.ShapeDtypeStruct((owners, groups, span, span), jnp.bfloat16)],
+        compiler_params=params(),
+        name="tables",
+    )(entries, angles)
+
+
+def run_mix(owner_of, place_of, received, take, give, blocks):
+    devices, sides, half, _ = received.shape
+    rows = 2 * half
+    unit = rows // devices
+    smem = pl.BlockSpec(memory_space=pltpu.SMEM)
+    hot_spec = pl.BlockSpec((1, sides, rows, rows), lambda i: (i, 0, 0, 0))
+    return pl.pallas_call(
+        mix_kernel,
+        grid=(devices,),
+        in_specs=[
+            smem,
+            smem,
+            pl.BlockSpec(received.shape, lambda i: (0, 0, 0, 0)),
+            hot_spec,
+            hot_spec,
+            pl.BlockSpec((1,) + blocks.shape[1:], lambda i: (i, 0, 0, 0)),
+        ],
+        out_specs=pl.BlockSpec((sides, devices, half, LANES), lambda i: (0, 0, 0, 0)),
+        out_shape=jax.ShapeDtypeStruct((sides, devices, half, LANES), jnp.bfloat16),
+        scratch_shapes=[
+            pltpu.VMEM((sides, devices, devices, unit, LANES), jnp.bfloat16),
+            pltpu.VMEM((sides, devices, devices, unit, LANES), jnp.bfloat16),
+        ],
+        compiler_params=params(),
+        name="mix",
+    )(owner_of, place_of, received, take, give, blocks)
+
+
+def unit_tables(entries, capacity, unit):
+    owners, sides, rows = entries.shape
+    ids = jnp.arange(owners, dtype=jnp.int32)
+    source = entries.reshape(owners, sides * rows) // capacity
+    counts = jnp.sum((source[None] == ids[:, None, None]).astype(jnp.int32), axis=2) // (unit * sides)
+    before = ids[:, None] < ids[None, :]
+    starts = jnp.sum(jnp.where(before[None], counts[:, :, None], 0), axis=1)
+    places = jnp.sum(jnp.where(before[:, :, None], counts[:, None, :], 0), axis=0)
+    inside = (starts[:, :, None] <= ids) & (ids < (starts + counts)[:, :, None])
+    owner_of = jnp.sum(jnp.where(inside, ids[None, :, None], 0), axis=1)
+    place_of = jnp.sum(jnp.where(inside, (places - starts)[:, :, None] + ids, 0), axis=1)
+    return owner_of, place_of
+
+
+def ranks(values):
+    return jnp.sum((values[:, :, None] < values[:, None, :]).astype(jnp.int32), axis=1)
+
+
+def tiled_local(messages, reverse_position, route_slot, atom_slots, angles, weights):
+    wide = lax.axis_size("wide")
+    narrow = lax.axis_size("narrow")
+    edge_rows, features = messages.shape
+    rows = edge_rows // wide
+    unit = rows // narrow
+    capacity = 2 * edge_rows // narrow
+    atoms = angles.shape[0]
+    back_rows = reverse_position.reshape(wide, rows)
+    current = messages.reshape(wide, rows, features)
+    received = lax.all_to_all(current, "wide", 0, 0, tiled=True)
+    rank = ranks(route_slot.reshape(wide, rows))
+    partner_rank = lax.all_to_all(rank, "wide", 0, 0, tiled=True)
+    hits = back_rows[:, :, None] == jnp.arange(rows, dtype=jnp.int32)
+    turned_rank = jnp.sum(jnp.where(hits, partner_rank[:, None, :], 0), axis=2)
+    listed = atom_slots.reshape(atoms // GROUP, GROUP, wide, SLOTS // wide)
+    listed = jnp.transpose(listed, (2, 0, 3, 1)).reshape(wide, rows)
+    entries = lax.all_gather(listed, "narrow", axis=0)
+    all_angles = lax.all_gather(angles, "narrow", axis=0)
+    owner_of, place_of = unit_tables(entries, capacity, unit)
+    take, give, blocks = run_tables(entries[:, :, None, :], all_angles)
+    back_rows = back_rows[:, None, :]
+    rank = rank[:, None, :]
+    turned_rank = turned_rank[:, None, :]
+    for section in range(BLOCKS):
+        if section:
+            received = lax.all_to_all(current, "wide", 0, 0, tiled=True)
+        second, packed = run_front(current, received, back_rows, rank, weights, section, narrow)
+        spread = lax.all_to_all(packed, "narrow", 0, 0, tiled=True)
+        mixed = run_mix(owner_of, place_of, spread, take, give, blocks)
+        flat = mixed.reshape(wide * narrow, rows // 2, LANES)
+        returned = lax.all_to_all(flat, ("wide", "narrow"), 0, 0, tiled=True)
+        returned = returned.reshape(wide, narrow, rows // 2, LANES)
+        current = run_back(second, returned, turned_rank, weights, section)
+    return current.reshape(edge_rows, features)
 
 
 def local(
@@ -83,21 +411,19 @@
         weight_expand,
         weight_reduce,
     )
-    edge_rows = messages.shape[0]
-    sub_rows = edge_rows // lax.axis_size("wide")
-    partner_rows = jnp.arange(edge_rows, dtype=jnp.int32) // sub_rows * sub_rows + reverse_position
-    mixing = angles.reshape(angles.shape[0], SLOTS, SLOTS)
-    current = messages
-    for section_index in range(BLOCKS):
-        reverse = reverse_edges(current, partner_rows)
-        second = edge_front(current, reverse, weights, section_index)
-        mixed_flat = owners_mix(second, route_slot, atom_slots, mixing)
-        returned = back_to_edges(mixed_flat, route_slot, atom_slots)
-        turned = None
-        turned, returned = (turned, returned)
-        turned = reverse_edges(returned, partner_rows)
-        current = edge_back(second, turned, weights, section_index)
-    return current
+    wide = lax.axis_size("wide")
+    narrow = lax.axis_size("narrow")
+    edge_rows, features = messages.shape
+    unit = edge_rows // wide // narrow
+    fits = (
+        features == narrow * HALF
+        and unit % 16 == 0
+        and narrow % 2 == 0
+        and angles.shape[0] % GROUP == 0
+        and (SLOTS // wide * GROUP) % 16 == 0
+    )
+    run = tiled_local if fits else general_local
+    return run(messages, reverse_position, route_slot, atom_slots, angles, weights)
 
 
 def solution(mesh):

time: 531 us -> 343 us (0.65); the launches traced: 523 us -> 343 us
  waiting for transfers between devices: 167 us -> 57.3 us
  Pallas kernels: 0 us -> 91.2 us
  local copies, waits for them, and re-layouts: 81.5 us -> 7.23 us
  matrix products: 50.7 us -> 0 us
  blocking collectives: 195 us -> 165 us
  other arithmetic: 10.6 us -> 1.42 us
    all_to_all x4, waiting for transfers between devices: 167 us -> 57.3 us  [the longest x1 38.3 us: tiled_local(): returned = lax.all_to_all(flat, ('wide', 'narrow'), 0, 0, tiled=True)]
    pallas_call x0 -> x7, Pallas kernels: none -> 91.2 us  [the longest x2 32.4 us: run_mix(): pl.pallas_call(mix_kernel, grid=(devices,), in_specs=[smem, smem, pl.Bloc...]
    all_to_all x4 -> x3, blocking collectives: 195 us -> 106 us  [the longest x1 41.4 us: tiled_local(): returned = lax.all_to_all(flat, ('wide', 'narrow'), 0, 0, tiled=True)]
    all_gather x0 -> x2, blocking collectives: none -> 59.2 us  [the longest x1 43.5 us: tiled_local(): entries = lax.all_gather(listed, 'narrow', axis=0)]
    dot_general x12 -> x0, matrix products: 50.7 us -> none  [the longest x10 49.6 us: project(): return jnp.dot(operand, weight, preferred_element_type=jnp.float32)]
    gather x8 -> x0, local copies, waits for them, and re-layouts: 41.6 us -> none  [the longest x4 19.8 us: reverse_edges(): return jnp.take(exchanged, partner_rows, axis=0)]
    scatter x4 -> x0, local copies, waits for them, and re-layouts: 38.1 us -> none  [the longest x2 19.1 us: back_to_edges(): jnp.zeros((buffer_rows, features), jnp.bfloat16).at[atom_slots]]
    select_n x6 -> x2, other arithmetic: 6.72 us -> 0.02 us  [the longest x1 0.01 us: unit_tables(): jnp.sum((source[None] == ids[:, None, None]).astype(jnp.int32), axis=2)]
  transfers between devices with their start and end apart: 4 -> 4, of which waited for: 4 -> 2; matrix products, arithmetic and copies ran while one was open for 2% -> 1% of each run, Pallas kernels for 0% -> 10%
where the time goes in v1:
time: 343 us
  blocking collectives  165 us (48%)
  Pallas kernels  91.2 us (27%)
  waiting for transfers between devices  57.3 us (17%)
  starting transfers between devices  20 us (6%)
  local copies, waits for them, and re-layouts  7.23 us (2%)
    all_gather x1, blocking collectives, tiled_local(): entries = lax.all_gather(listed, 'narrow', axis=0)  43.5 us
    all_to_all x1, blocking collectives, tiled_local(): returned = lax.all_to_all(flat, ('wide', 'narrow'), 0, 0, tiled=True)  41.4 us
    all_to_all x1, blocking collectives, tiled_local(): spread = lax.all_to_all(packed, 'narrow', 0, 0, tiled=True)  41.3 us
    all_to_all x1, waiting for transfers between devices, tiled_local(): returned = lax.all_to_all(flat, ('wide', 'narrow'), 0, 0, tiled=True)  38.3 us
    pallas_call x2, Pallas kernels, run_mix(): pl.pallas_call(mix_kernel, grid=(devices,), in_specs=[smem, smem, pl.Bloc...  32.4 us
    all_to_all x1, blocking collectives, tiled_local(): received = lax.all_to_all(current, 'wide', 0, 0, tiled=True)  23.3 us
    pallas_call x2, Pallas kernels, run_front(): pl.pallas_call(front_kernel, grid=(sides,), in_specs=[edge_spec, edge_spe...  21.8 us
    pallas_call x2, Pallas kernels, run_back(): pl.pallas_call(back_kernel, grid=(sides,), in_specs=[edge_spec, pl.BlockS...  19.6 us
  transfers between devices with their start and end apart: 4, of which 2 were waited for; matrix products, arithmetic and copies ran while one was open for 1% of the time, Pallas kernels for 10%

profile of v1, /device:TPU:0, one launch (start us, length us, event | category | flops | bytes accessed | tf_op | source)
XLA Modules:
  0.0 342.6 jit_solution(13204806791930414229)
XLA Ops:
  0.0 5.3 %all-to-all-start = ((bf16[4,384,512]{2,1,0:T(8,128)(2,1)}), bf16[4,384,512]{2,1,0:T(8,128)(2,1)}, u32[]{:S(2)}, u32[]{:S(2)}) async-start(bf16[4,384,512]{2,1,0:T(8,128)(2,1)} %bitcast.21), calls=%async_computation | async-start | bytes 3145728 | tf_op jit(solution)/shard_map/all_to_all | solution.py:362
  5.4 0.3 convert_reduce_fusion
  5.7 0.6 broadcast_in_dim.90.rank_ref
  6.3 19.0 %all-to-all-done.recv_ref = bf16[4,384,512]{2,1,0:T(8,128)(2,1)} async-done(((bf16[4,384,512]{2,1,0:T(8,128)(2,1)}), bf16[4,384,512]{2,1,0:T(8,128)(2,1)}, u32[]{:S(2)}, u32[]{:S(2)}) %all-to-all-start) | async-done | bytes 1572896 | tf_op jit(solution)/shard_map/all_to_all | solution.py:362
  25.3 1.2 copy-done.4
  26.6 1.2 copy-done.6
  27.8 1.2 copy-done.8
  29.0 10.9 %front.2 = (bf16[4,384,512]{2,1,0:T(8,128)(2,1)}, bf16[8,4,192,128]{3,2,1,0:T(8,128)(2,1)}) custom-call(bf16[4,384,512]{2,1,0:T(8,128)(2,1)} %bitcast.22, bf16[4,384,512]{2,1,0:T(8,128)(2,1)} %all-to-all-done.recv_ref, s32[4,1,384]{2,1,0:T(1,128)S(1)} %broadcast_in_dim_reshape.2.back_ref, s32[4,1,384]{2,1,0:T(1,128)} %broadcast_in_dim.90.rank_ref, ...), custom_call_target="tpu_custom_call" | custom-call | tf_op jit(solution)/shard_map/front/pallas_call | solution.py:248
  39.9 5.2 %all-to-all-start.1 = ((bf16[8,4,192,128]{3,2,1,0:T(8,128)(2,1)}), bf16[8,4,192,128]{3,2,1,0:T(8,128)(2,1)S(1)}, u32[]{:S(2)}, u32[]{:S(2)}) async-start(bf16[8,4,192,128]{3,2,1,0:T(8,128)(2,1)} %get-tuple-element.13), calls=%async_computation.1 | async-start | bytes 3145728 | tf_op jit(solution)/shard_map/all_to_all | solution.py:380
  45.1 0.1 reshape.113
  45.3 0.1 copy.16
  45.4 0.1 all_gather_reshape.3
  45.5 43.5 %all_gather.9 = s32[8,4,384]{2,1,0:T(4,128)S(1)} all-gather(s32[1,4,384]{2,1,0:T(4,128)S(1)} %all_gather_reshape.3), channel_id=1, replica_groups=mesh['wide'=4,'narrow'=8] {'narrow'}, dimensions={0}, use_global_device_ids=true | all-gather | bytes 55296 | tf_op jit(solution)/shard_map/all_gather | solution.py:369
  89.2 0.2 convert_reduce_fusion.1
  89.4 0.1 select_reduce_fusion.2
  89.5 15.7 %all-gather = bf16[384,1024]{1,0:T(8,128)(2,1)S(1)} all-gather(bf16[48,1024]{1,0:T(8,128)(2,1)} %param.17), channel_id=2, replica_groups=mesh['wide'=4,'narrow'=8] {'narrow'}, dimensions={0}, use_global_device_ids=true | all-gather | bytes 884736 | tf_op jit(solution)/shard_map/all_gather | solution.py:370
  105.2 3.2 all-to-all-start.3
  108.4 0.1 select_reduce_fusion.1
  108.6 17.4 %tables.1 = (bf16[8,4,384,384]{3,2,1,0:T(8,128)(2,1)}, bf16[8,4,384,384]{3,2,1,0:T(8,128)(2,1)}, bf16[8,6,256,256]{3,2,1,0:T(8,128)(2,1)}) custom-call(s32[8,4,1,384]{3,2,1,0:T(1,128)S(1)} %broadcast_in_dim.97.entry_ref, bf16[8,48,1024]{2,1,0:T(8,128)(2,1)S(1)} %bitcast.20), custom_call_target="tpu_custom_call" | custom-call | tf_op jit(solution)/shard_map/tables/pallas_call | solution.py:292
  126.0 16.7 %mix.2 = bf16[4,8,192,128]{3,2,1,0:T(8,128)(2,1)} custom-call(s32[8,8]{1,0:T(8,128)S(1)} %get-tuple-element.20.owner_ref, s32[8,8]{1,0:T(8,128)S(1)} %get-tuple-element.19.place_ref, bf16[8,4,192,128]{3,2,1,0:T(8,128)(2,1)S(1)} %all-to-all-done.1.recv_ref, bf16[8,4,384,384]{3,2,1,0:T(8,128)(2,1)} %get-tuple-element.14.take_ref, ...), custom_call_target="tpu_custom_call" | custom-call | tf_op jit(solution)/shard_map/mix/pallas_call | solution.py:312
  142.7 6.2 %all-to-all-start.2 = ((bf16[32,192,128]{2,1,0:T(8,128)(2,1)}), bf16[32,192,128]{2,1,0:T(8,128)(2,1)}, u32[]{:S(2)}, u32[]{:S(2)}) async-start(bf16[32,192,128]{2,1,0:T(8,128)(2,1)} %bitcast.3), calls=%async_computation.2 | async-start | bytes 3145728 | tf_op jit(solution)/shard_map/all_to_all | solution.py:383
  149.0 0.6 select_reduce_fusion
  149.5 38.3 %all-to-all-done.2 = bf16[32,192,128]{2,1,0:T(8,128)(2,1)} async-done(((bf16[32,192,128]{2,1,0:T(8,128)(2,1)}), bf16[32,192,128]{2,1,0:T(8,128)(2,1)}, u32[]{:S(2)}, u32[]{:S(2)}) %all-to-all-start.2) | async-done | bytes 1572896 | tf_op jit(solution)/shard_map/all_to_all | solution.py:383
  187.8 1.2 copy-done.11
  189.0 1.2 copy-done.13
  190.3 9.5 %back.2.cur_ref = bf16[4,384,512]{2,1,0:T(8,128)(2,1)S(1)} custom-call(bf16[4,384,512]{2,1,0:T(8,128)(2,1)} %get-tuple-element.12.second_ref, bf16[4,8,192,128]{3,2,1,0:T(8,128)(2,1)} %bitcast.4.packed_ref, s32[4,1,384]{2,1,0:T(1,128)S(1)} %broadcast_in_dim.101.rank_ref, bf16[2,512,512]{2,1,0:T(8,128)(2,1)S(1)} %copy-done.10, ...), custom_call_target="tpu_custom_call" | custom-call | tf_op jit(solution)/shard_map/back/pallas_call | solution.py:269
  199.9 23.3 %all_to_all.36.recv_ref = bf16[4,384,512]{2,1,0:T(8,128)(2,1)} all-to-all(bf16[4,384,512]{2,1,0:T(8,128)(2,1)S(1)} %back.2.cur_ref), channel_id=1, replica_groups=mesh['wide'=4,'narrow'=8] {'wide'}, dimensions={0} | all-to-all | bytes 3145728 | tf_op jit(solution)/shard_map/all_to_all | solution.py:378
  223.2 10.9 %front.3 = (bf16[4,384,512]{2,1,0:T(8,128)(2,1)}, bf16[8,4,192,128]{3,2,1,0:T(8,128)(2,1)}) custom-call(bf16[4,384,512]{2,1,0:T(8,128)(2,1)} %copy-done, bf16[4,384,512]{2,1,0:T(8,128)(2,1)} %all_to_all.36.recv_ref, s32[4,1,384]{2,1,0:T(1,128)S(1)} %broadcast_in_dim_reshape.2.back_ref, s32[4,1,384]{2,1,0:T(1,128)} %broadcast_in_dim.90.rank_ref, ...), custom_call_target="tpu_custom_call" | custom-call | tf_op jit(solution)/shard_map/front/pallas_call | solution.py:248
  234.1 41.3 %all_to_all.37.recv_ref = bf16[8,4,192,128]{3,2,1,0:T(8,128)(2,1)S(1)} all-to-all(bf16[8,4,192,128]{3,2,1,0:T(8,128)(2,1)} %get-tuple-element.18), channel_id=1, replica_groups=mesh['wide'=4,'narrow'=8] {'narrow'}, dimensions={0} | all-to-all | bytes 3145728 | tf_op jit(solution)/shard_map/all_to_all | solution.py:380
  275.5 15.7 %mix.3 = bf16[4,8,192,128]{3,2,1,0:T(8,128)(2,1)S(1)} custom-call(s32[8,8]{1,0:T(8,128)S(1)} %get-tuple-element.20.owner_ref, s32[8,8]{1,0:T(8,128)S(1)} %get-tuple-element.19.place_ref, bf16[8,4,192,128]{3,2,1,0:T(8,128)(2,1)S(1)} %all_to_all.37.recv_ref, bf16[8,4,384,384]{3,2,1,0:T(8,128)(2,1)} %get-tuple-element.14.take_ref, ...), custom_call_target="tpu_custom_call" | custom-call | tf_op jit(solution)/shard_map/mix/pallas_call | solution.py:312
  291.2 41.4 %all_to_all.38 = bf16[32,192,128]{2,1,0:T(8,128)(2,1)} all-to-all(bf16[32,192,128]{2,1,0:T(8,128)(2,1)S(1)} %bitcast.19), channel_id=1, replica_groups=mesh['wide'=4,'narrow'=8] {'wide','narrow'}, dimensions={0} | all-to-all | bytes 3145728 | tf_op jit(solution)/shard_map/all_to_all | solution.py:383
  332.6 10.1 %back.3 = bf16[4,384,512]{2,1,0:T(8,128)(2,1)} custom-call(bf16[4,384,512]{2,1,0:T(8,128)(2,1)S(1)} %copy-done.15, bf16[4,8,192,128]{3,2,1,0:T(8,128)(2,1)} %bitcast.23, s32[4,1,384]{2,1,0:T(1,128)S(1)} %broadcast_in_dim.101.rank_ref, bf16[2,512,512]{2,1,0:T(8,128)(2,1)S(1)} %copy-done.10, bf16[2,512,512]{2,1,0:T(8,128)(2,1)S(1)} %copy-done.12, ...), custom_call_target="tpu_custom_call" | custom-call | tf_op jit(solution)/shard_map/back/pallas_call | solution.py:269
  (49 shorter events, 0.3 us)
Async XLA Ops:
  0.0 5.3 %copy-start.16 = (s32[1536]{0:T(1024)S(1)}, s32[1536]{0:T(1024)}, u32[]{:S(2)}) copy-start(s32[1536]{0:T(1024)} %param.14) | copy-start | bytes 18436
  0.0 5.3 %copy-start.17 = (s32[1536]{0:T(1024)S(1)}, s32[1536]{0:T(1024)}, u32[]{:S(2)}) copy-start(s32[1536]{0:T(1024)} %param.15) | copy-start | bytes 18436
  0.0 25.3 %copy-start.1 = (bf16[2,512,512]{2,1,0:T(8,128)(2,1)S(1)}, bf16[2,512,512]{2,1,0:T(8,128)(2,1)}, u32[]{:S(2)}) copy-start(bf16[2,512,512]{2,1,0:T(8,128)(2,1)} %wm.3) | copy-start | bytes 3145732
  0.0 25.3 %copy-start.2 = (bf16[2,512,512]{2,1,0:T(8,128)(2,1)S(1)}, bf16[2,512,512]{2,1,0:T(8,128)(2,1)}, u32[]{:S(2)}) copy-start(bf16[2,512,512]{2,1,0:T(8,128)(2,1)} %wr.3) | copy-start | bytes 3145732
  0.0 25.3 %all-to-all-start = ((bf16[4,384,512]{2,1,0:T(8,128)(2,1)}), bf16[4,384,512]{2,1,0:T(8,128)(2,1)}, u32[]{:S(2)}, u32[]{:S(2)}) async-start(bf16[4,384,512]{2,1,0:T(8,128)(2,1)} %bitcast.21), calls=%async_computation | async-start | bytes 3145728 | tf_op jit(solution)/shard_map/all_to_all | solution.py:362
  25.3 1.2 copy-start.4
  26.6 1.2 copy-start.6
  27.8 1.2 copy-start.8
  39.9 5.2 %copy-start.18 = (s32[1536]{0:T(1024)S(1)}, s32[1536]{0:T(1024)}, u32[]{:S(2)}) copy-start(s32[1536]{0:T(1024)} %param.16) | copy-start | bytes 18436
  39.9 65.4 %all-to-all-start.1 = ((bf16[8,4,192,128]{3,2,1,0:T(8,128)(2,1)}), bf16[8,4,192,128]{3,2,1,0:T(8,128)(2,1)S(1)}, u32[]{:S(2)}, u32[]{:S(2)}) async-start(bf16[8,4,192,128]{3,2,1,0:T(8,128)(2,1)} %get-tuple-element.13), calls=%async_computation.1 | async-start | bytes 3145728 | tf_op jit(solution)/shard_map/all_to_all | solution.py:380
  105.2 37.5 %all-to-all-start.3 = ((s32[4,1,384]{2,1,0:T(1,128)}), s32[4,1,384]{2,1,0:T(1,128)S(1)}, u32[]{:S(2)}, u32[]{:S(2)}) async-start(s32[4,1,384]{2,1,0:T(1,128)} %broadcast_in_dim.90.rank_ref), calls=%async_computation.3 | async-start | bytes 12288 | tf_op jit(solution)/shard_map/all_to_all | solution.py:364
  142.7 45.1 %copy-start.10 = (bf16[2,512,512]{2,1,0:T(8,128)(2,1)S(1)}, bf16[2,512,512]{2,1,0:T(8,128)(2,1)}, u32[]{:S(2)}) copy-start(bf16[2,512,512]{2,1,0:T(8,128)(2,1)} %wl.3) | copy-start | bytes 3145732
  142.7 45.1 %all-to-all-start.2 = ((bf16[32,192,128]{2,1,0:T(8,128)(2,1)}), bf16[32,192,128]{2,1,0:T(8,128)(2,1)}, u32[]{:S(2)}, u32[]{:S(2)}) async-start(bf16[32,192,128]{2,1,0:T(8,128)(2,1)} %bitcast.3), calls=%async_computation.2 | async-start | bytes 3145728 | tf_op jit(solution)/shard_map/all_to_all | solution.py:383
  187.8 1.2 copy-start.11
  189.0 1.2 copy-start.13
  190.3 32.9 %copy-start.9 = (bf16[2,512,512]{2,1,0:T(8,128)(2,1)S(1)}, bf16[2,512,512]{2,1,0:T(8,128)(2,1)}, u32[]{:S(2)}) copy-start(bf16[2,512,512]{2,1,0:T(8,128)(2,1)} %wo.3) | copy-start | bytes 3145732
  199.8 23.4 %copy-start = (bf16[4,384,512]{2,1,0:T(8,128)(2,1)}, bf16[4,384,512]{2,1,0:T(8,128)(2,1)S(1)}, u32[]{:S(2)}) copy-start(bf16[4,384,512]{2,1,0:T(8,128)(2,1)S(1)} %back.2.cur_ref) | copy-start | bytes 4718596
  199.8 23.4 %copy-start.3 = (bf16[2,512,512]{2,1,0:T(8,128)(2,1)S(1)}, bf16[2,512,512]{2,1,0:T(8,128)(2,1)}, u32[]{:S(2)}) copy-start(bf16[2,512,512]{2,1,0:T(8,128)(2,1)} %wr.3) | copy-start | bytes 3145732
  199.8 23.4 %copy-start.5 = (bf16[2,512,512]{2,1,0:T(8,128)(2,1)S(1)}, bf16[2,512,512]{2,1,0:T(8,128)(2,1)}, u32[]{:S(2)}) copy-start(bf16[2,512,512]{2,1,0:T(8,128)(2,1)} %wc.3) | copy-start | bytes 3145732
  199.8 23.3 %copy-start.7 = (bf16[2,512,512]{2,1,0:T(8,128)(2,1)S(1)}, bf16[2,512,512]{2,1,0:T(8,128)(2,1)}, u32[]{:S(2)}) copy-start(bf16[2,512,512]{2,1,0:T(8,128)(2,1)} %wi.3) | copy-start | bytes 3145732
  275.5 57.1 %copy-start.15 = (bf16[4,384,512]{2,1,0:T(8,128)(2,1)S(1)}, bf16[4,384,512]{2,1,0:T(8,128)(2,1)}, u32[]{:S(2)}) copy-start(bf16[4,384,512]{2,1,0:T(8,128)(2,1)} %get-tuple-element.17.second_ref) | copy-start | bytes 4718596
  291.2 41.4 %copy-start.12 = (bf16[2,512,512]{2,1,0:T(8,128)(2,1)S(1)}, bf16[2,512,512]{2,1,0:T(8,128)(2,1)}, u32[]{:S(2)}) copy-start(bf16[2,512,512]{2,1,0:T(8,128)(2,1)} %we.3) | copy-start | bytes 3145732
  291.2 41.4 %copy-start.14 = (bf16[2,512,512]{2,1,0:T(8,128)(2,1)S(1)}, bf16[2,512,512]{2,1,0:T(8,128)(2,1)}, u32[]{:S(2)}) copy-start(bf16[2,512,512]{2,1,0:T(8,128)(2,1)} %wd.3) | copy-start | bytes 3145732
